TPU v7x, 128 devices: a whole 4x4x4 slice. The times are simulated.
128 devices in a mesh: gx: 8 (over y, core), gy: 16 (over x, z).
Axes of the slice: x: 4, y: 4, z: 4, core: 2. Of those that a mesh axis runs over, the one named last changes fastest.
Arguments:
- tokens_in: bfloat16 [16384, 1024], P(('gx', 'gy')), may hold values from -64 to 64
- dest_slot: int32 [16384], P(('gx', 'gy')), may hold values from 0 to 16383, as said below
- w_query: bfloat16 [1024, 1024], replicated, may hold values from -1.5 to 1.5
- w_key: bfloat16 [1024, 1024], replicated, may hold values from -0.75 to 0.75
- w_value: bfloat16 [1024, 1024], replicated, may hold values from -0.1875 to 0.1875
- surrogate: bfloat16 [1024], replicated, may hold values from -4 to 4
- gain_cluster: float32 [1024], replicated, may hold values from 0.25 to 1.75
- gain_summary: float32 [1024], replicated, may hold values from 0.25 to 1.75
- w_out: bfloat16 [1024, 1024], replicated, may hold values from -0.1875 to 0.1875
Outputs:
- layer_out: bfloat16 [16384, 1024], P(('gx', 'gy'))
Inputs may be any that keep to these rules, and one draw needn't show every extreme that they name: dest_slot is a permutation of the 16384 slots, so every cluster has exactly 128 members. Slot s lies on device s // 128, which thus holds exactly 128 slots. Of the 128 tokens of one device at most 2 have slots on any one device, and in every draw, the device at mesh position (gx, gy) has exactly 2 tokens with slots on the device at ((gx + 4) % 8, gy).
All inputs are finite; a program needn't handle non-finite values.
Results may differ from a plain program's by a relative error of at most 0.011.
Values may be sent and summed in bfloat16 or wider, within the bound.
A program may use at most 64 MiB of HBM per device.

v0:
```python
import math

import jax
import jax.numpy as jnp
from jax import lax
from jax.sharding import PartitionSpec as P

HEADS = 16
CSIZE = 128


def rms_scale(values, gain_vec):
    mean_sq = jnp.mean(values * values, axis=-1, keepdims=True)
    return values * lax.rsqrt(mean_sq + 1e-06) * gain_vec


def project(row_data, weight):
    return jnp.dot(row_data, weight, preferred_element_type=jnp.float32).astype(jnp.bfloat16)


def cluster_work(q_rows, k_rows, v_rows, surrogate, gain_cluster):
    row_total, model_width = q_rows.shape
    groups = row_total // CSIZE
    head_dim = model_width // HEADS
    scaling = 1.0 / math.sqrt(head_dim)
    query_heads = q_rows.reshape(groups, CSIZE, HEADS, head_dim)
    key_heads = k_rows.reshape(groups, CSIZE, HEADS, head_dim)
    value_heads = v_rows.reshape(groups, CSIZE, HEADS, head_dim)
    scores = (
        jnp.einsum("cihd,cjhd->chij", query_heads, key_heads, preferred_element_type=jnp.float32)
        * scaling
    )
    attn_probs = jax.nn.softmax(scores, axis=-1).astype(jnp.bfloat16)
    attended = jnp.einsum(
        "chij,cjhd->cihd", attn_probs, value_heads, preferred_element_type=jnp.float32
    ).reshape(row_total, model_width)
    branch = rms_scale(attended, gain_cluster).astype(jnp.bfloat16)
    anchor = surrogate.reshape(HEADS, head_dim)
    logits = (
        jnp.einsum("cihd,hd->chi", key_heads, anchor, preferred_element_type=jnp.float32) * scaling
    )
    pooled = jax.nn.softmax(logits, axis=-1).astype(jnp.bfloat16)
    key_sum = jnp.einsum("chi,cihd->chd", pooled, key_heads, preferred_element_type=jnp.float32)
    value_summary = jnp.einsum(
        "chi,cihd->chd", pooled, value_heads, preferred_element_type=jnp.float32
    ).astype(jnp.bfloat16)
    mean_sq = jnp.mean(key_sum * key_sum, axis=-1, keepdims=True)
    key_summary = (key_sum * lax.rsqrt(mean_sq + 1e-06)).astype(jnp.bfloat16)
    return (
        branch,
        key_summary.reshape(groups, model_width),
        value_summary.reshape(groups, model_width),
    )


def summary_attention(q_rows, key_summary, value_summary, gain_summary):
    row_total, model_width = q_rows.shape
    head_dim = model_width // HEADS
    scaling = 1.0 / math.sqrt(head_dim)
    query_heads = q_rows.reshape(row_total, HEADS, head_dim)
    key_piece = lax.all_gather(key_summary, ("gx", "gy"), axis=0, tiled=True)
    value_piece = lax.all_gather(value_summary, ("gx", "gy"), axis=0, tiled=True)
    run_max = jnp.full((HEADS, row_total), -1e30, jnp.float32)
    run_acc = jnp.zeros((row_total, HEADS, head_dim), jnp.float32)
    piece_rows = key_piece.shape[0]
    key_heads = key_piece.reshape(piece_rows, HEADS, head_dim)
    value_heads = value_piece.reshape(piece_rows, HEADS, head_dim)
    logits = (
        jnp.einsum("thd,chd->htc", query_heads, key_heads, preferred_element_type=jnp.float32)
        * scaling
    )
    new_max = jnp.maximum(run_max, jnp.max(logits, axis=-1))
    rescale = jnp.exp(run_max - new_max)
    weights = jnp.exp(logits - new_max[:, :, None])
    run_sum = jnp.sum(weights, axis=-1)
    added = jnp.einsum(
        "htc,chd->thd",
        weights.astype(jnp.bfloat16),
        value_heads,
        preferred_element_type=jnp.float32,
    )
    run_acc = run_acc * rescale.T[:, :, None] + added
    run_max, run_sum, run_acc = (new_max, run_sum, run_acc)
    summary_att = (run_acc / run_sum.T[:, :, None]).reshape(row_total, model_width)
    return rms_scale(summary_att, gain_summary)


def body(
    tokens_in, dest_slot, w_query, w_key, w_value, surrogate, gain_cluster, gain_summary, w_out
):
    shards = lax.axis_size(("gx", "gy"))
    local_rows, model_width = tokens_in.shape
    capacity = 2 * local_rows // shards
    owner_dev = dest_slot // local_rows
    target = dest_slot - owner_dev * local_rows
    member = (owner_dev[:, None] == jnp.arange(shards, dtype=jnp.int32)[None, :]).astype(jnp.int32)
    before = jnp.sum((jnp.cumsum(member, axis=0) - member) * member, axis=1)
    position = owner_dev * capacity + before
    source = (
        jnp.full((shards * capacity,), local_rows, jnp.int32)
        .at[position]
        .set(jnp.arange(local_rows, dtype=jnp.int32))
    )
    slot_sent = jnp.take(target, source, axis=0, mode="fill", fill_value=local_rows).reshape(
        shards, capacity
    )

    def pack_rows(row_data):
        return jnp.take(row_data, source, axis=0, mode="fill", fill_value=0).reshape(
            shards, capacity, model_width
        )

    q_rows = project(tokens_in, w_query)
    k_rows = project(tokens_in, w_key)
    v_rows = project(tokens_in, w_value)
    q_got, k_got, v_got, slot_got = (
        lax.all_to_all(pack_rows(q_rows), ("gx", "gy"), split_axis=0, concat_axis=0, tiled=True),
        lax.all_to_all(pack_rows(k_rows), ("gx", "gy"), split_axis=0, concat_axis=0, tiled=True),
        lax.all_to_all(pack_rows(v_rows), ("gx", "gy"), split_axis=0, concat_axis=0, tiled=True),
        lax.all_to_all(slot_sent, ("gx", "gy"), split_axis=0, concat_axis=0, tiled=True),
    )
    flat_slots = slot_got.reshape(-1)
    order_in = (
        jnp.zeros((local_rows,), jnp.int32)
        .at[flat_slots]
        .set(jnp.arange(flat_slots.shape[0], dtype=jnp.int32), mode="drop")
    )
    flat_slots, order_in = (flat_slots, order_in)
    branch, key_summary, value_summary = cluster_work(
        q_got.reshape(-1, model_width)[order_in],
        k_got.reshape(-1, model_width)[order_in],
        v_got.reshape(-1, model_width)[order_in],
        surrogate,
        gain_cluster,
    )
    returned = lax.all_to_all(
        jnp.take(branch, flat_slots, axis=0, mode="fill", fill_value=0).reshape(
            shards, capacity, model_width
        ),
        ("gx", "gy"),
        split_axis=0,
        concat_axis=0,
        tiled=True,
    )
    branch_rows = returned.reshape(-1, model_width)[position]
    summary = summary_attention(q_rows, key_summary, value_summary, gain_summary)
    mixture = (branch_rows.astype(jnp.float32) + summary).astype(jnp.bfloat16)
    return jnp.dot(mixture, w_out, preferred_element_type=jnp.float32).astype(jnp.bfloat16)


def solution(mesh):
    in_specs = (P(("gx", "gy"), None), P(("gx", "gy")), P(), P(), P(), P(), P(), P(), P())
    out_specs = P(("gx", "gy"), None)
    return jax.shard_map(body, mesh=mesh, in_specs=in_specs, out_specs=out_specs, check_vma=False)
```

profile of v0, /device:TPU:1, one launch (start us, length us, event | category | flops | bytes accessed | tf_op | source)
XLA Modules:
  0.0 224.4 jit_solution(5349197438471258772)
XLA Ops:
  2.3 1.9 gather_fusion
  4.9 11.5 %all-to-all-start.1 = ((s32[128,1,2]{2,1,0:T(1,128)}), s32[128,1,2]{2,1,0:T(1,128)S(1)}, u32[]{:S(2)}, u32[]{:S(2)}) async-start(s32[128,1,2]{2,1,0:T(1,128)} %bitcast), calls=%async_computation.1 | async-start | bytes 131072 | tf_op jit(solution)/shard_map/all_to_all | solution.py:120
  16.4 1.4 convolution_convert_fusion.2
  17.9 1.2 gather_fusion.6
  19.0 2.0 convolution_convert_fusion.1
  21.1 2.0 gather_fusion.7
  23.0 2.0 convolution_convert_fusion.3
  25.1 2.0 gather_fusion.5
  27.1 2.4 %broadcast_select_fusion.2 = (bf16[256,1024]{1,0:T(8,128)(2,1)}, bf16[256,1024]{1,0:T(8,128)(2,1)}, bf16[256,1024]{1,0:T(8,128)(2,1)S(1)}) fusion(bf16[256,1024]{1,0:T(8,128)(2,1)S(1)} %gather_fusion.6, pred[256]{0:T(512)(128)(4,1)S(1)} %get-tuple-element.7, bf16[256,1024]{1,0:T(8,128)(2,1)} %gather_fusion.7, bf16[256,1024]{1,0:T(8,128)(2,1)} %gather_fusion.5), kind=kLoop, calls=%fused_computation.36 | loop fusion | flops 786432 | bytes 3145984 | tf_op jit(solution)/shard_map/jit(_take)/select_n | solution.py:109
  30.4 2.0 reshape.227
  32.4 2.0 reshape.230
  34.4 1.0 reshape.223
  35.5 9.8 %all-to-all-start.2 = ((bf16[128,2,1024]{2,1,0:T(2,128)(2,1)}), bf16[128,2,1024]{2,1,0:T(2,128)(2,1)S(1)}, u32[]{:S(2)}, u32[]{:S(2)}) async-start(bf16[128,2,1024]{2,1,0:T(2,128)(2,1)} %reshape.227), calls=%async_computation.2 | async-start | bytes 1048576 | tf_op jit(solution)/shard_map/all_to_all | solution.py:117
  46.9 1.4 scatter_custom_fusion.1
  48.3 10.4 %all-to-all-done.2 = bf16[128,2,1024]{2,1,0:T(2,128)(2,1)S(1)} async-done(((bf16[128,2,1024]{2,1,0:T(2,128)(2,1)}), bf16[128,2,1024]{2,1,0:T(2,128)(2,1)S(1)}, u32[]{:S(2)}, u32[]{:S(2)}) %all-to-all-start.2) | async-done | bytes 524320 | tf_op jit(solution)/shard_map/all_to_all | solution.py:117
  58.6 5.7 %all-to-all-start.3 = ((bf16[128,2,1024]{2,1,0:T(2,128)(2,1)}), bf16[128,2,1024]{2,1,0:T(2,128)(2,1)}, u32[]{:S(2)}, u32[]{:S(2)}) async-start(bf16[128,2,1024]{2,1,0:T(2,128)(2,1)} %reshape.230), calls=%async_computation.3 | async-start | bytes 1048576 | tf_op jit(solution)/shard_map/all_to_all | solution.py:118
  66.3 11.2 %all-to-all-done.3 = bf16[128,2,1024]{2,1,0:T(2,128)(2,1)} async-done(((bf16[128,2,1024]{2,1,0:T(2,128)(2,1)}), bf16[128,2,1024]{2,1,0:T(2,128)(2,1)}, u32[]{:S(2)}, u32[]{:S(2)}) %all-to-all-start.3) | async-done | bytes 524320 | tf_op jit(solution)/shard_map/all_to_all | solution.py:118
  77.6 4.7 %all-to-all-start = ((bf16[128,2,1024]{2,1,0:T(2,128)(2,1)}), bf16[128,2,1024]{2,1,0:T(2,128)(2,1)S(1)}, u32[]{:S(2)}, u32[]{:S(2)}) async-start(bf16[128,2,1024]{2,1,0:T(2,128)(2,1)} %reshape.223), calls=%async_computation | async-start | bytes 1048576 | tf_op jit(solution)/shard_map/all_to_all | solution.py:119
  82.2 1.2 reshape.231
  85.7 54.6 %all-gather = bf16[128,1,1024]{2,1,0:T(2,128)(2,1)S(1)} all-gather(bf16[1,1,1024]{2,1,0:T(2,128)(2,1)S(1)} %reshape.342), channel_id=1, replica_groups=mesh['gx'=8,'gy'=16] {'gx','gy'}, dimensions={0}, use_global_device_ids=true | all-gather | bytes 264192 | tf_op jit(solution)/shard_map/all_gather | solution.py:61
  140.7 1.5 fusion.27
  142.2 2.4 %convolution_multiply_fusion.1 = f32[16,128,128]{1,2,0:T(8,128)} fusion(bf16[128,16,64]{0,2,1:T(8,128)(2,1)} %bitcast.60, bf16[128,16,64]{0,2,1:T(8,128)(2,1)} %bitcast.64), kind=kOutput, calls=%fused_computation.15 | convolution fusion | flops 33816576 | bytes 1572864 | tf_op jit(solution)/shard_map/cihd,cjhd->chij/dot_general | solution.py:30
  146.2 1.9 fusion.8
  148.5 1.2 gather_fusion.8
  150.8 6.3 %all-to-all-start.4 = ((bf16[128,2,1024]{2,1,0:T(2,128)(2,1)}), bf16[128,2,1024]{2,1,0:T(2,128)(2,1)}, u32[]{:S(2)}, u32[]{:S(2)}) async-start(bf16[128,2,1024]{2,1,0:T(2,128)(2,1)} %reshape.235), calls=%async_computation.4 | async-start | bytes 1048576 | tf_op jit(solution)/shard_map/all_to_all | solution.py:136
  157.1 1.3 fusion.26
  158.6 57.2 %all-gather.1 = bf16[128,1,1024]{2,1,0:T(2,128)(2,1)} all-gather(bf16[1,1,1024]{2,1,0:T(2,128)(2,1)S(1)} %reshape.344), channel_id=1, replica_groups=mesh['gx'=8,'gy'=16] {'gx','gy'}, dimensions={0}, use_global_device_ids=true | all-gather | bytes 264192 | tf_op jit(solution)/shard_map/all_gather | solution.py:62
  215.8 1.3 copy.47
  217.1 1.1 multiply_reduce_fusion
  218.2 1.2 copy.49
  219.5 1.2 reshape.236
  221.6 2.8 %convolution_convert_fusion = bf16[128,1024]{1,0:T(8,128)(2,1)} fusion(bf16[1024,1024]{1,0:T(8,128)(2,1)} %param.19, f32[128,1024]{1,0:T(8,128)S(1)} %copy.49, bf16[128,1024]{1,0:T(8,128)(2,1)S(1)} %gather_fusion.4, f32[1024]{0:T(1024)S(1)} %copy-done.4, f32[128]{0:T(128)S(1)} %add_rsqrt_fusion), kind=kOutput, calls=%fused_computation.19 | convolution fusion | flops 269221888 | bytes 3150336 | tf_op jit(solution)/shard_map/dot_general | solution.py:148
  (70 shorter events, 14.1 us)
Async XLA Ops:
  0.0 16.4 %copy-start = (bf16[1024,1024]{1,0:T(8,128)(2,1)S(1)}, bf16[1024,1024]{1,0:T(8,128)(2,1)}, u32[]{:S(2)}) copy-start(bf16[1024,1024]{1,0:T(8,128)(2,1)} %param.13) | copy-start | bytes 6291460
  4.9 30.5 %all-to-all-start.1 = ((s32[128,1,2]{2,1,0:T(1,128)}), s32[128,1,2]{2,1,0:T(1,128)S(1)}, u32[]{:S(2)}, u32[]{:S(2)}) async-start(s32[128,1,2]{2,1,0:T(1,128)} %bitcast), calls=%async_computation.1 | async-start | bytes 131072 | tf_op jit(solution)/shard_map/all_to_all | solution.py:120
  17.9 1.2 copy-start.1
  27.1 3.2 %copy-start.5 = (bf16[1024]{0:T(1024)(128)(2,1)S(1)}, bf16[1024]{0:T(1024)(128)(2,1)}, u32[]{:S(2)}) copy-start(bf16[1024]{0:T(1024)(128)(2,1)} %param.16) | copy-start | bytes 6148
  35.5 23.2 %all-to-all-start.2 = ((bf16[128,2,1024]{2,1,0:T(2,128)(2,1)}), bf16[128,2,1024]{2,1,0:T(2,128)(2,1)S(1)}, u32[]{:S(2)}, u32[]{:S(2)}) async-start(bf16[128,2,1024]{2,1,0:T(2,128)(2,1)} %reshape.227), calls=%async_computation.2 | async-start | bytes 1048576 | tf_op jit(solution)/shard_map/all_to_all | solution.py:117
  58.6 18.9 %all-to-all-start.3 = ((bf16[128,2,1024]{2,1,0:T(2,128)(2,1)}), bf16[128,2,1024]{2,1,0:T(2,128)(2,1)}, u32[]{:S(2)}, u32[]{:S(2)}) async-start(bf16[128,2,1024]{2,1,0:T(2,128)(2,1)} %reshape.230), calls=%async_computation.3 | async-start | bytes 1048576 | tf_op jit(solution)/shard_map/all_to_all | solution.py:118
  77.6 67.0 %all-to-all-start = ((bf16[128,2,1024]{2,1,0:T(2,128)(2,1)}), bf16[128,2,1024]{2,1,0:T(2,128)(2,1)S(1)}, u32[]{:S(2)}, u32[]{:S(2)}) async-start(bf16[128,2,1024]{2,1,0:T(2,128)(2,1)} %reshape.223), calls=%async_computation | async-start | bytes 1048576 | tf_op jit(solution)/shard_map/all_to_all | solution.py:119
  84.5 1.0 copy-start.2
  146.2 2.2 copy-start.3
  150.8 68.7 %all-to-all-start.4 = ((bf16[128,2,1024]{2,1,0:T(2,128)(2,1)}), bf16[128,2,1024]{2,1,0:T(2,128)(2,1)}, u32[]{:S(2)}, u32[]{:S(2)}) async-start(bf16[128,2,1024]{2,1,0:T(2,128)(2,1)} %reshape.235), calls=%async_computation.4 | async-start | bytes 1048576 | tf_op jit(solution)/shard_map/all_to_all | solution.py:136
  218.2 3.4 %copy-start.4 = (f32[1024]{0:T(1024)S(1)}, f32[1024]{0:T(1024)}, u32[]{:S(2)}) copy-start(f32[1024]{0:T(1024)} %param.18) | copy-start | bytes 12292
where the time goes:
time: 225 us; the launch traced here: 224 us
  blocking collectives  112 us (50%)
  starting transfers between devices  38 us (17%)
  local copies, waits for them, and re-layouts  30 us (13%)
  waiting for transfers between devices  21.6 us (10%)
  matrix products  17.2 us (8%)
  other arithmetic  5.42 us (2%)
    all_gather x1, blocking collectives, summary_attention(): lax.all_gather(value_summary, ('gx', 'gy'), axis=0, tiled=True)  57.2 us
    all_gather x1, blocking collectives, summary_attention(): key_piece = lax.all_gather(key_summary, ('gx', 'gy'), axis=0, tiled=True)  54.6 us
    all_to_all x1, starting transfers between devices, body(): lax.all_to_all(slot_sent, ('gx', 'gy'), split_axis=0, concat_axis=0, tile...  11.5 us
    all_to_all x1, waiting for transfers between devices, body(): lax.all_to_all(pack_rows(k_rows), ('gx', 'gy'), split_axis=0, concat_axis...  11.2 us
    all_to_all x1, waiting for transfers between devices, body(): lax.all_to_all(pack_rows(q_rows), ('gx', 'gy'), split_axis=0, concat_axis...  10.4 us
    all_to_all x1, starting transfers between devices, body(): lax.all_to_all(pack_rows(q_rows), ('gx', 'gy'), split_axis=0, concat_axis...  9.76 us
    all_to_all x1, starting transfers between devices, body(): lax.all_to_all(jnp.take(branch, flat_slots, axis=0, mode='fill', fill_val...  6.35 us
    all_to_all x1, starting transfers between devices, body(): lax.all_to_all(pack_rows(k_rows), ('gx', 'gy'), split_axis=0, concat_axis...  5.72 us
  transfers between devices with their start and end apart: 5, of which 2 were waited for; matrix products, arithmetic and copies ran while one was open for 16% of the time, Pallas kernels for 0%

commit v1 on v0

v1 whole, which is shorter than its diff:
```python
import functools
import math

import jax
import jax.numpy as jnp
from jax import lax
from jax.experimental import pallas as pl
from jax.experimental.pallas import tpu as pltpu
from jax.sharding import PartitionSpec as P

MESH = pl.DeviceIdType.MESH
F32, BF16 = jnp.float32, jnp.bfloat16
GX, GY = 8, 16
N = GX * GY
T = 128
D = 1024
HEADS, HD = 16, 64
PAIRS = D // 128
CAP = 2
ROWS = N * CAP
PAD = 128.0
MARK = 1024.0
EXP2_SCALE = math.log2(math.e) / math.sqrt(HD)


def iota(shape, dim):
    return lax.broadcasted_iota(jnp.int32, shape, dim).astype(F32)


def dot(a, b):
    return jnp.dot(a, b, preferred_element_type=F32)


def dot_nt(a, b):
    return lax.dot_general(a, b, (((1,), (1,)), ((), ())), preferred_element_type=F32)


def dot_tn(a, b):
    return lax.dot_general(a, b, (((0,), (0,)), ((), ())), preferred_element_type=F32)


def attend_pair(q_tile, k_tile, v_tile, low):
    zero = jnp.zeros_like(q_tile)
    q_two = jnp.concatenate([jnp.where(low, q_tile, zero), jnp.where(low, zero, q_tile)], axis=0)
    scores = dot_nt(q_two, k_tile)
    top = jnp.max(scores, axis=1, keepdims=True)
    raised = jnp.exp2((scores - top) * EXP2_SCALE)
    total = 1.0 / jnp.sum(raised, axis=1, keepdims=True)
    raised = raised.astype(BF16)
    both = jnp.concatenate([raised[:T], raised[T:]], axis=1)
    v_two = jnp.concatenate([jnp.where(low, v_tile, zero), jnp.where(low, zero, v_tile)], axis=0)
    return dot(both, v_two) * jnp.where(low, total[:T], total[T:])


def kernel(
    x_ref, slot_ref, surr_ref, gain_c_ref, gain_s_ref, wq_hbm, wk_hbm, wv_hbm, wo_hbm,
    out_ref,
    wq, wk, wv, wo, stage, rows, send_buf, recv_buf, back_buf, home_buf, sum_buf, sums_buf, att, q_loc,
    w_sem, fwd_send, fwd_recv, sum_send, sum_recv, back_send, back_recv, row_sem,
):
    gx, gy = lax.axis_index("gx"), lax.axis_index("gy")
    me = gx * GY + gy

    loads = [
        pltpu.make_async_copy(src, dst, w_sem.at[i])
        for i, (src, dst) in enumerate(((wq_hbm, wq), (wk_hbm, wk), (wv_hbm, wv), (wo_hbm, wo)))
    ]
    for load in loads:
        load.start()

    with jax.named_scope("barrier_a"):
        barrier = pltpu.get_barrier_semaphore()
        for i in range(1, GX):
            pl.semaphore_signal(barrier, inc=1, device_id=(lax.rem(gx + i, GX), gy), device_id_type=MESH)
        for i in range(1, GY):
            pl.semaphore_signal(barrier, inc=1, device_id=(gx, lax.rem(gy + i, GY)), device_id_type=MESH)

    with jax.named_scope("pack"):
        owner_row = (slot_ref[...] >> 7).astype(F32)
        sub, lane = iota((T, T), 0), iota((T, T), 1)
        owner_wide = jnp.broadcast_to(owner_row, (T, T))
        owner_col = jnp.sum(jnp.where(sub == lane, owner_wide, 0.0), axis=1, keepdims=True)
        same = (owner_col == owner_wide).astype(F32)
        place_row = owner_row * CAP + jnp.sum(jnp.where(sub < lane, same, 0.0), axis=0, keepdims=True)
        place_col = owner_col * CAP + jnp.sum(jnp.where(lane < sub, same, 0.0), axis=1, keepdims=True)
        pick = (iota((ROWS, T), 0) == place_row).astype(F32)
        filled = jnp.sum(pick, axis=1, keepdims=True) > 0.5
        pick = pick.astype(BF16)
        for j in range(PAIRS):
            part = dot(pick, x_ref[:, j * 128 : (j + 1) * 128])
            stage[pl.ds(j, ROWS, stride=8), :] = jnp.where(filled, part, PAD)
        send_buf[...] = stage[...].astype(BF16).reshape(N, 16, 128)

    with jax.named_scope("barrier_b"):
        pl.semaphore_wait(barrier, GX + GY - 2)
        for i in range(1, GX):
            pl.semaphore_signal(row_sem, inc=1, device_id=(lax.rem(gx + i, GX), gy), device_id_type=MESH)
        pl.semaphore_wait(row_sem, GX - 1)

    def to_all(src_of, dst, send_sem, recv_sem):
        def send(i, carry):
            tx = lax.rem(gx + i // GY, GX)
            ty = lax.rem(gy + lax.rem(i, GY), GY)
            pltpu.make_async_remote_copy(
                src_ref=src_of(tx * GY + ty),
                dst_ref=dst.at[me],
                send_sem=send_sem,
                recv_sem=recv_sem,
                device_id=(tx, ty),
                device_id_type=MESH,
            ).start()
            return carry

        lax.fori_loop(1, N, send, 0)

    def wait_all(buf, sem):
        some = buf.at[pl.ds(0, N - 1)]
        pltpu.make_async_copy(some, some, sem).wait()

    with jax.named_scope("send_tokens"):
        to_all(lambda d: send_buf.at[d], recv_buf, fwd_send, fwd_recv)
    recv_buf[pl.ds(me, 1)] = send_buf[pl.ds(me, 1)]

    with jax.named_scope("local_query"):
        loads[0].wait()
        q_loc[...] = dot(x_ref[...], wq[...]).astype(BF16)

    def unpack(buf):
        stage[...] = buf[...].astype(F32).reshape(ROWS * 8, 128)
        for j in range(PAIRS):
            rows[:, j * 128 : (j + 1) * 128] = stage[pl.ds(j, ROWS, stride=8), :].astype(BF16)

    with jax.named_scope("wait_tokens"):
        wait_all(recv_buf, fwd_recv)
    with jax.named_scope("unpack"):
        unpack(recv_buf)
        real = (rows[:, :128].astype(F32) < 100.0).astype(BF16)
        r_sub, r_lane = iota((ROWS, ROWS), 0), iota((ROWS, ROWS), 1)
        mark = jnp.where(r_sub == r_lane, -MARK, 0.0)
        rank_row = dot_tn(real, (mark + (r_sub < r_lane).astype(F32)).astype(BF16))
        rank_col = dot((mark + (r_lane < r_sub).astype(F32)).astype(BF16), real)
        gather = (rank_row == iota((T, ROWS), 0) - MARK).astype(BF16)
        scatter = (rank_col == iota((ROWS, T), 1) - MARK).astype(BF16)
        members = dot(gather, rows[...]).astype(BF16)

    with jax.named_scope("key_value"):
        loads[1].wait()
        key = dot(members, wk[...]).astype(BF16)
        loads[2].wait()
        value = dot(members, wv[...]).astype(BF16)

    with jax.named_scope("summary"):
        own = lax.broadcasted_iota(jnp.int32, (HEADS, D), 1) // HD == lax.broadcasted_iota(
            jnp.int32, (HEADS, D), 0
        )
        anchor = jnp.where(own, jnp.broadcast_to(surr_ref[...].astype(F32), (HEADS, D)), 0.0).astype(BF16)
        logits = dot_nt(anchor, key)
        raised = jnp.exp2((logits - jnp.max(logits, axis=1, keepdims=True)) * EXP2_SCALE)
        pooled = (raised / jnp.sum(raised, axis=1, keepdims=True)).astype(BF16)
        key_sum = jnp.where(own, dot(pooled, key), 0.0)
        key_sum = key_sum * lax.rsqrt(jnp.sum(key_sum * key_sum, axis=1, keepdims=True) / HD + 1e-6)
        key_sum = jnp.sum(key_sum, axis=0, keepdims=True)
        value_sum = jnp.sum(jnp.where(own, dot(pooled, value), 0.0), axis=0, keepdims=True)
        for j in range(PAIRS):
            stage[j : j + 1, :] = key_sum[:, j * 128 : (j + 1) * 128]
            stage[8 + j : 9 + j, :] = value_sum[:, j * 128 : (j + 1) * 128]
        sum_buf[...] = stage[:16, :].astype(BF16)
    with jax.named_scope("send_summary"):
        to_all(lambda d: sum_buf, sums_buf, sum_send, sum_recv)
    sums_buf[pl.ds(me, 1)] = sum_buf[...][None]

    low = lax.broadcasted_iota(jnp.int32, (T, 128), 1) < HD

    with jax.named_scope("query"):
        query = dot(members, wq[...]).astype(BF16)
    with jax.named_scope("attend"):
        square = jnp.zeros((T, 128), F32)
        for j in range(PAIRS):
            at = slice(j * 128, (j + 1) * 128)
            got = attend_pair(query[:, at], key[:, at], value[:, at], low)
            square = square + got * got
            att[:, at] = got
        scale = lax.rsqrt(jnp.sum(square, axis=1, keepdims=True) / D + 1e-6)
        branch = (att[...] * scale * gain_c_ref[...]).astype(BF16)
    with jax.named_scope("pack_back"):
        for j in range(PAIRS):
            stage[pl.ds(j, ROWS, stride=8), :] = dot(scatter, branch[:, j * 128 : (j + 1) * 128])
        back_buf[...] = stage[...].astype(BF16).reshape(N, 16, 128)
    with jax.named_scope("send_back"):
        to_all(lambda d: back_buf.at[d], home_buf, back_send, back_recv)
    home_buf[pl.ds(me, 1)] = back_buf[pl.ds(me, 1)]

    with jax.named_scope("wait_summary"):
        wait_all(sums_buf, sum_recv)
    with jax.named_scope("attend_summary"):
        stage[...] = sums_buf[...].astype(F32).reshape(N * 16, 128)
        square = jnp.zeros((T, 128), F32)
        for j in range(PAIRS):
            at = slice(j * 128, (j + 1) * 128)
            got = attend_pair(
                q_loc[:, at],
                stage[pl.ds(j, N, stride=16), :].astype(BF16),
                stage[pl.ds(8 + j, N, stride=16), :].astype(BF16),
                low,
            )
            square = square + got * got
            att[:, at] = got
        scale = lax.rsqrt(jnp.sum(square, axis=1, keepdims=True) / D + 1e-6)
        att[...] = att[...] * scale * gain_s_ref[...]

    with jax.named_scope("wait_back"):
        wait_all(home_buf, back_recv)
    with jax.named_scope("mix_out"):
        unpack(home_buf)
        pick_back = (iota((T, ROWS), 1) == place_col).astype(BF16)
        mixture = (dot(pick_back, rows[...]) + att[...]).astype(BF16)
        loads[3].wait()
        out_ref[...] = dot(mixture, wo[...]).astype(BF16)

    with jax.named_scope("drain"):
        wait_all(send_buf, fwd_send)
        wait_all(sums_buf, sum_send)
        wait_all(back_buf, back_send)


def body(
    tokens_in, dest_slot, w_query, w_key, w_value, surrogate, gain_cluster, gain_summary, w_out
):
    vmem, hbm = pl.BlockSpec(memory_space=pltpu.VMEM), pl.BlockSpec(memory_space=pl.ANY)
    tiles = pltpu.VMEM((N, 16, 128), BF16)
    weight = pltpu.VMEM((D, D), BF16)
    dma = pltpu.SemaphoreType.DMA
    return pl.pallas_call(
        kernel,
        out_shape=jax.ShapeDtypeStruct((T, D), BF16),
        in_specs=[vmem] * 5 + [hbm] * 4,
        out_specs=vmem,
        scratch_shapes=[weight] * 4
        + [
            pltpu.VMEM((ROWS * 8, 128), F32),
            pltpu.VMEM((ROWS, D), BF16),
            tiles, tiles, tiles, tiles,
            pltpu.VMEM((16, 128), BF16),
            tiles,
            pltpu.VMEM((T, D), F32),
            pltpu.VMEM((T, D), BF16),
            dma((4,)), dma, dma, dma, dma, dma, dma,
            pltpu.SemaphoreType.REGULAR,
        ],
        compiler_params=pltpu.CompilerParams(
            collective_id=0, has_side_effects=True, vmem_limit_bytes=60 * 2**20
        ),
    )(
        tokens_in,
        dest_slot.reshape(1, T),
        surrogate.reshape(1, D),
        gain_cluster.reshape(1, D),
        gain_summary.reshape(1, D),
        w_query, w_key, w_value, w_out,
    )


def solution(mesh):
    in_specs = (P(("gx", "gy"), None), P(("gx", "gy")), P(), P(), P(), P(), P(), P(), P())
    out_specs = P(("gx", "gy"), None)
    return jax.shard_map(body, mesh=mesh, in_specs=in_specs, out_specs=out_specs, check_vma=False)
```

time: 225 us -> 44.3 us (0.20)
  blocking collectives: 112 us -> 0 us
  Pallas kernels: 0 us -> 41.2 us
  starting transfers between devices: 38 us -> 0 us
  local copies, waits for them, and re-layouts: 30 us -> 2.95 us
  waiting for transfers between devices: 21.6 us -> 0 us
  matrix products: 17.2 us -> 0 us
  other arithmetic: 5.42 us -> 0 us
    all_gather x2 -> x0, blocking collectives: 112 us -> none  [the longest x1 57.2 us: summary_attention(): lax.all_gather(value_summary, ('gx', 'gy'), axis=0, tiled=True)]
    pallas_call x0 -> x1, Pallas kernels: none -> 41.2 us  [body(): pl.pallas_call(kernel, out_shape=jax.ShapeDtypeStruct((T, D), BF16), in_s...]
    all_to_all x5 -> x0, starting transfers between devices: 38 us -> none  [the longest x1 11.5 us: body(): lax.all_to_all(slot_sent, ('gx', 'gy'), split_axis=0, concat_axis=0, tile...]
    all_to_all x5 -> x0, waiting for transfers between devices: 21.6 us -> none  [the longest x1 11.2 us: body(): lax.all_to_all(pack_rows(k_rows), ('gx', 'gy'), split_axis=0, concat_axis...]
    dot_general x11 -> x0, matrix products: 15.7 us -> none  [the longest x3 5.47 us: project(): jnp.dot(row_data, weight, preferred_element_type=jnp.float32)]
    gather x12 -> x0, local copies, waits for them, and re-layouts: 12.8 us -> none  [the longest x3 5.11 us: pack_rows(): jnp.take(row_data, source, axis=0, mode='fill', fill_value=0)]
    reshape x13 -> x1, local copies, waits for them, and re-layouts: 10.8 us -> 1.28 us  [body(): surrogate.reshape(1, D)]
    select_n x8 -> x0, other arithmetic: 2.5 us -> none  [the longest x1 2.36 us: pack_rows(): jnp.take(row_data, source, axis=0, mode='fill', fill_value=0)]
  transfers between devices with their start and end apart: 5 -> 0, of which waited for: 2 -> 0; matrix products, arithmetic and copies ran while one was open for 16% -> 0% of each run, Pallas kernels for 0% -> 0%
where the time goes in v1:
time: 44.3 us; the launch traced here: 44.1 us
  Pallas kernels  41.2 us (93%)
  local copies, waits for them, and re-layouts  2.95 us (7%)
    pallas_call x1, Pallas kernels, body(): pl.pallas_call(kernel, out_shape=jax.ShapeDtypeStruct((T, D), BF16), in_s...  41.2 us
    unnamed x1, local copies, waits for them, and re-layouts  1.67 us
    reshape x1, local copies, waits for them, and re-layouts, body(): surrogate.reshape(1, D)  1.28 us

profile of v1, /device:TPU:1, one launch (start us, length us, event | category | flops | bytes accessed | tf_op | source)
XLA Modules:
  0.0 44.1 jit_solution(13901465549109668796)
XLA Ops:
  0.0 1.3 %reshape.13.surr_ref = bf16[1,1024]{1,0:T(2,128)(2,1)} reshape(bf16[1024]{0:T(1024)(128)(2,1)} %param.14) | data formatting | bytes 4096 | tf_op jit(solution)/shard_map/reshape | solution.py:256
  1.3 41.2 %shard_map.91 = bf16[128,1024]{1,0:T(8,128)(2,1)} custom-call(bf16[128,1024]{1,0:T(8,128)(2,1)} %x_ref.1, s32[1,128]{1,0:T(1,128)} %bitcast.5, bf16[1,1024]{1,0:T(2,128)(2,1)} %reshape.13.surr_ref, f32[1,1024]{1,0:T(1,128)} %bitcast.3, f32[1,1024]{1,0:T(1,128)} %bitcast.4, bf16[1024,1024]{1,0:T(8,128)(2,1)} %wq_hbm.1, bf16[1024,1024]{1,0:T(8,128)(2,1)} %wk_hbm.1, ...), custom_call_target="tpu_custom_call" | custom-call | tf_op jit(solution)/shard_map/pallas_call | solution.py:233
  42.5 1.7 %copy.11 = bf16[128,1024]{1,0:T(8,128)(2,1)} copy(bf16[128,1024]{1,0:T(8,128)(2,1)} %shard_map.91) | data formatting | bytes 524288

commit v2 on v1

--- a/solution.py
+++ b/solution.py
@@ -12,6 +12,7 @@
 F32, BF16 = jnp.float32, jnp.bfloat16
 GX, GY = 8, 16
 N = GX * GY
+CHIPS = N // 2
 T = 128
 D = 1024
 HEADS, HD = 16, 64
@@ -53,19 +54,29 @@
 
 
 def kernel(
-    x_ref, slot_ref, surr_ref, gain_c_ref, gain_s_ref, wq_hbm, wk_hbm, wv_hbm, wo_hbm,
+    x_hbm, slot_hbm, surr_hbm, gain_c_hbm, gain_s_hbm, wq_hbm, wk_hbm, wv_hbm, wo_hbm,
     out_ref,
-    wq, wk, wv, wo, stage, rows, send_buf, recv_buf, back_buf, home_buf, sum_buf, sums_buf, att, q_loc,
-    w_sem, fwd_send, fwd_recv, sum_send, sum_recv, back_send, back_recv, row_sem,
+    x_ref, slot_ref, surr_ref, gain_c_ref, gain_s_ref, wq, wk, wv, wo, stage, rows, send_buf, recv_buf, back_buf, home_buf, sum_buf, sums_buf, att, q_loc,
+    x_sem, w_sem, fwd_send, fwd_recv, sum_send, sum_recv, pass_send, pass_recv, back_send, back_recv, row_sem,
 ):
     gx, gy = lax.axis_index("gx"), lax.axis_index("gy")
     me = gx * GY + gy
 
+    y, core = gx // 2, lax.rem(gx, 2)
+    firsts = [
+        pltpu.make_async_copy(src, dst, x_sem.at[i])
+        for i, (src, dst) in enumerate(((slot_hbm, slot_ref), (x_hbm, x_ref)))
+    ]
     loads = [
         pltpu.make_async_copy(src, dst, w_sem.at[i])
-        for i, (src, dst) in enumerate(((wq_hbm, wq), (wk_hbm, wk), (wv_hbm, wv), (wo_hbm, wo)))
+        for i, (src, dst) in enumerate(
+            (
+                (wq_hbm, wq), (wk_hbm, wk), (wv_hbm, wv), (wo_hbm, wo),
+                (surr_hbm, surr_ref), (gain_c_hbm, gain_c_ref), (gain_s_hbm, gain_s_ref),
+            )
+        )
     ]
-    for load in loads:
+    for load in firsts:
         load.start()
 
     with jax.named_scope("barrier_a"):
@@ -76,6 +87,10 @@
             pl.semaphore_signal(barrier, inc=1, device_id=(gx, lax.rem(gy + i, GY)), device_id_type=MESH)
 
     with jax.named_scope("pack"):
+        for load in firsts:
+            load.wait()
+        for load in loads:
+            load.start()
         owner_row = (slot_ref[...] >> 7).astype(F32)
         sub, lane = iota((T, T), 0), iota((T, T), 1)
         owner_wide = jnp.broadcast_to(owner_row, (T, T))
@@ -113,9 +128,12 @@
 
         lax.fori_loop(1, N, send, 0)
 
+    def wait_for(buf, count, sem):
+        some = buf.at[pl.ds(0, count)]
+        pltpu.make_async_copy(some, some, sem).wait()
+
     def wait_all(buf, sem):
-        some = buf.at[pl.ds(0, N - 1)]
-        pltpu.make_async_copy(some, some, sem).wait()
+        wait_for(buf, N - 1, sem)
 
     with jax.named_scope("send_tokens"):
         to_all(lambda d: send_buf.at[d], recv_buf, fwd_send, fwd_recv)
@@ -153,7 +171,10 @@
         own = lax.broadcasted_iota(jnp.int32, (HEADS, D), 1) // HD == lax.broadcasted_iota(
             jnp.int32, (HEADS, D), 0
         )
-        anchor = jnp.where(own, jnp.broadcast_to(surr_ref[...].astype(F32), (HEADS, D)), 0.0).astype(BF16)
+        loads[4].wait()
+        surr = surr_ref[...].astype(F32)
+        surr = jnp.concatenate([surr[j : j + 1] for j in range(PAIRS)], axis=1)
+        anchor = jnp.where(own, jnp.broadcast_to(surr, (HEADS, D)), 0.0).astype(BF16)
         logits = dot_nt(anchor, key)
         raised = jnp.exp2((logits - jnp.max(logits, axis=1, keepdims=True)) * EXP2_SCALE)
         pooled = (raised / jnp.sum(raised, axis=1, keepdims=True)).astype(BF16)
@@ -166,8 +187,23 @@
             stage[8 + j : 9 + j, :] = value_sum[:, j * 128 : (j + 1) * 128]
         sum_buf[...] = stage[:16, :].astype(BF16)
     with jax.named_scope("send_summary"):
-        to_all(lambda d: sum_buf, sums_buf, sum_send, sum_recv)
-    sums_buf[pl.ds(me, 1)] = sum_buf[...][None]
+        mine = core * CHIPS + y * GY + gy
+        for dy in range(4):
+
+            def send(i, carry, dy=dy):
+                tx, ty = lax.rem(gx + 2 * dy, GX), lax.rem(gy + i, GY)
+                pltpu.make_async_remote_copy(
+                    src_ref=sum_buf,
+                    dst_ref=sums_buf.at[mine],
+                    send_sem=sum_send,
+                    recv_sem=sum_recv.at[dy],
+                    device_id=(tx, ty),
+                    device_id_type=MESH,
+                ).start()
+                return carry
+
+            lax.fori_loop(1 if dy == 0 else 0, GY, send, 0)
+        sums_buf[pl.ds(mine, 1)] = sum_buf[...][None]
 
     low = lax.broadcasted_iota(jnp.int32, (T, 128), 1) < HD
 
@@ -181,6 +217,7 @@
             square = square + got * got
             att[:, at] = got
         scale = lax.rsqrt(jnp.sum(square, axis=1, keepdims=True) / D + 1e-6)
+        loads[5].wait()
         branch = (att[...] * scale * gain_c_ref[...]).astype(BF16)
     with jax.named_scope("pack_back"):
         for j in range(PAIRS):
@@ -190,8 +227,24 @@
         to_all(lambda d: back_buf.at[d], home_buf, back_send, back_recv)
     home_buf[pl.ds(me, 1)] = back_buf[pl.ds(me, 1)]
 
-    with jax.named_scope("wait_summary"):
-        wait_all(sums_buf, sum_recv)
+    with jax.named_scope("pass_summary"):
+        passes = []
+        for dy in range(4):
+            wait_for(sums_buf, GY - 1 if dy == 0 else GY, sum_recv.at[dy])
+            block = sums_buf.at[pl.ds(core * CHIPS + lax.rem(y + 4 - dy, 4) * GY, GY)]
+            passes.append(
+                pltpu.make_async_remote_copy(
+                    src_ref=block,
+                    dst_ref=block,
+                    send_sem=pass_send.at[dy],
+                    recv_sem=pass_recv.at[dy],
+                    device_id=(gx + 1 - 2 * core, gy),
+                    device_id_type=MESH,
+                )
+            )
+            passes[-1].start()
+        for one in passes:
+            one.wait()
     with jax.named_scope("attend_summary"):
         stage[...] = sums_buf[...].astype(F32).reshape(N * 16, 128)
         square = jnp.zeros((T, 128), F32)
@@ -206,6 +259,7 @@
             square = square + got * got
             att[:, at] = got
         scale = lax.rsqrt(jnp.sum(square, axis=1, keepdims=True) / D + 1e-6)
+        loads[6].wait()
         att[...] = att[...] * scale * gain_s_ref[...]
 
     with jax.named_scope("wait_back"):
@@ -219,7 +273,7 @@
 
     with jax.named_scope("drain"):
         wait_all(send_buf, fwd_send)
-        wait_all(sums_buf, sum_send)
+        wait_for(sums_buf, CHIPS - 1, sum_send)
         wait_all(back_buf, back_send)
 
 
@@ -233,9 +287,16 @@
     return pl.pallas_call(
         kernel,
         out_shape=jax.ShapeDtypeStruct((T, D), BF16),
-        in_specs=[vmem] * 5 + [hbm] * 4,
+        in_specs=[hbm] * 9,
         out_specs=vmem,
-        scratch_shapes=[weight] * 4
+        scratch_shapes=[
+            pltpu.VMEM((T, D), BF16),
+            pltpu.VMEM((1, T), jnp.int32),
+            pltpu.VMEM((PAIRS, 128), BF16),
+            pltpu.VMEM((1, D), F32),
+            pltpu.VMEM((1, D), F32),
+        ]
+        + [weight] * 4
         + [
             pltpu.VMEM((ROWS * 8, 128), F32),
             pltpu.VMEM((ROWS, D), BF16),
@@ -244,7 +305,7 @@
             tiles,
             pltpu.VMEM((T, D), F32),
             pltpu.VMEM((T, D), BF16),
-            dma((4,)), dma, dma, dma, dma, dma, dma,
+            dma((2,)), dma((7,)), dma, dma, dma, dma((4,)), dma((4,)), dma((4,)), dma, dma,
             pltpu.SemaphoreType.REGULAR,
         ],
         compiler_params=pltpu.CompilerParams(
@@ -253,7 +314,7 @@
     )(
         tokens_in,
         dest_slot.reshape(1, T),
-        surrogate.reshape(1, D),
+        surrogate.reshape(PAIRS, 128),
         gain_cluster.reshape(1, D),
         gain_summary.reshape(1, D),
         w_query, w_key, w_value, w_out,

time: 44.3 us -> 39.2 us (0.88)
  Pallas kernels: 41.2 us -> 37.4 us
  local copies, waits for them, and re-layouts: 2.95 us -> 1.67 us
    pallas_call x1, Pallas kernels: 41.2 us -> 37.4 us  [body(): pl.pallas_call(kernel, out_shape=jax.ShapeDtypeStruct((T, D), BF16), in_s...]
    reshape x1 -> x0, local copies, waits for them, and re-layouts: 1.28 us -> none  [body(): surrogate.reshape(1, D)]
where the time goes in v2:
time: 39.2 us; the launch traced here: 39 us
  Pallas kernels  37.4 us (95%)
  local copies, waits for them, and re-layouts  1.67 us (4%)
    pallas_call x1, Pallas kernels, body(): pl.pallas_call(kernel, out_shape=jax.ShapeDtypeStruct((T, D), BF16), in_s...  37.4 us
    unnamed x1, local copies, waits for them, and re-layouts  1.67 us

profile of v2, /device:TPU:1, one launch (start us, length us, event | category | flops | bytes accessed | tf_op | source)
XLA Modules:
  0.0 39.0 jit_solution(16298705178887021365)
XLA Ops:
  0.0 37.4 %shard_map.91 = bf16[128,1024]{1,0:T(8,128)(2,1)} custom-call(bf16[128,1024]{1,0:T(8,128)(2,1)} %x_hbm.1, s32[1,128]{1,0:T(1,128)} %bitcast.7, bf16[8,128]{1,0:T(8,128)(2,1)} %bitcast.6, f32[1,1024]{1,0:T(1,128)} %bitcast.4, f32[1,1024]{1,0:T(1,128)} %bitcast.5, bf16[1024,1024]{1,0:T(8,128)(2,1)} %wq_hbm.1, bf16[1024,1024]{1,0:T(8,128)(2,1)} %wk_hbm.1, ...), custom_call_target="tpu_custom_call" | custom-call | tf_op jit(solution)/shard_map/pallas_call | solution.py:287
  37.4 1.7 %copy.11 = bf16[128,1024]{1,0:T(8,128)(2,1)} copy(bf16[128,1024]{1,0:T(8,128)(2,1)} %shard_map.91) | data formatting | bytes 524288

commit v3 on v2

--- a/solution.py
+++ b/solution.py
@@ -54,9 +54,9 @@
 
 
 def kernel(
-    x_hbm, slot_hbm, surr_hbm, gain_c_hbm, gain_s_hbm, wq_hbm, wk_hbm, wv_hbm, wo_hbm,
+    x_hbm, slot_hbm, surr_hbm, gain_c_hbm, gain_s_hbm, wq_hbm, wk_hbm, wv_hbm,
     out_ref,
-    x_ref, slot_ref, surr_ref, gain_c_ref, gain_s_ref, wq, wk, wv, wo, stage, rows, send_buf, recv_buf, back_buf, home_buf, sum_buf, sums_buf, att, q_loc,
+    x_ref, slot_ref, surr_ref, gain_c_ref, gain_s_ref, wq, wk, wv, stage, rows, send_buf, recv_buf, back_buf, home_buf, sum_buf, sums_buf, att, q_loc,
     x_sem, w_sem, fwd_send, fwd_recv, sum_send, sum_recv, pass_send, pass_recv, back_send, back_recv, row_sem,
 ):
     gx, gy = lax.axis_index("gx"), lax.axis_index("gy")
@@ -71,7 +71,7 @@
         pltpu.make_async_copy(src, dst, w_sem.at[i])
         for i, (src, dst) in enumerate(
             (
-                (wq_hbm, wq), (wk_hbm, wk), (wv_hbm, wv), (wo_hbm, wo),
+                (wq_hbm, wq), (wk_hbm, wk), (wv_hbm, wv),
                 (surr_hbm, surr_ref), (gain_c_hbm, gain_c_ref), (gain_s_hbm, gain_s_ref),
             )
         )
@@ -171,7 +171,7 @@
         own = lax.broadcasted_iota(jnp.int32, (HEADS, D), 1) // HD == lax.broadcasted_iota(
             jnp.int32, (HEADS, D), 0
         )
-        loads[4].wait()
+        loads[3].wait()
         surr = surr_ref[...].astype(F32)
         surr = jnp.concatenate([surr[j : j + 1] for j in range(PAIRS)], axis=1)
         anchor = jnp.where(own, jnp.broadcast_to(surr, (HEADS, D)), 0.0).astype(BF16)
@@ -217,7 +217,7 @@
             square = square + got * got
             att[:, at] = got
         scale = lax.rsqrt(jnp.sum(square, axis=1, keepdims=True) / D + 1e-6)
-        loads[5].wait()
+        loads[4].wait()
         branch = (att[...] * scale * gain_c_ref[...]).astype(BF16)
     with jax.named_scope("pack_back"):
         for j in range(PAIRS):
@@ -259,7 +259,7 @@
             square = square + got * got
             att[:, at] = got
         scale = lax.rsqrt(jnp.sum(square, axis=1, keepdims=True) / D + 1e-6)
-        loads[6].wait()
+        loads[5].wait()
         att[...] = att[...] * scale * gain_s_ref[...]
 
     with jax.named_scope("wait_back"):
@@ -268,8 +268,7 @@
         unpack(home_buf)
         pick_back = (iota((T, ROWS), 1) == place_col).astype(BF16)
         mixture = (dot(pick_back, rows[...]) + att[...]).astype(BF16)
-        loads[3].wait()
-        out_ref[...] = dot(mixture, wo[...]).astype(BF16)
+        out_ref[...] = mixture
 
     with jax.named_scope("drain"):
         wait_all(send_buf, fwd_send)
@@ -284,10 +283,10 @@
     tiles = pltpu.VMEM((N, 16, 128), BF16)
     weight = pltpu.VMEM((D, D), BF16)
     dma = pltpu.SemaphoreType.DMA
-    return pl.pallas_call(
+    mixture = pl.pallas_call(
         kernel,
         out_shape=jax.ShapeDtypeStruct((T, D), BF16),
-        in_specs=[hbm] * 9,
+        in_specs=[hbm] * 8,
         out_specs=vmem,
         scratch_shapes=[
             pltpu.VMEM((T, D), BF16),
@@ -296,7 +295,7 @@
             pltpu.VMEM((1, D), F32),
             pltpu.VMEM((1, D), F32),
         ]
-        + [weight] * 4
+        + [weight] * 3
         + [
             pltpu.VMEM((ROWS * 8, 128), F32),
             pltpu.VMEM((ROWS, D), BF16),
@@ -305,20 +304,26 @@
             tiles,
             pltpu.VMEM((T, D), F32),
             pltpu.VMEM((T, D), BF16),
-            dma((2,)), dma((7,)), dma, dma, dma, dma((4,)), dma((4,)), dma((4,)), dma, dma,
+            dma((2,)), dma((6,)), dma, dma, dma, dma((4,)), dma((4,)), dma((4,)), dma, dma,
             pltpu.SemaphoreType.REGULAR,
         ],
         compiler_params=pltpu.CompilerParams(
-            collective_id=0, has_side_effects=True, vmem_limit_bytes=60 * 2**20
+            collective_id=0, has_side_effects=True, vmem_limit_bytes=40 * 2**20
         ),
     )(
-        tokens_in,
-        dest_slot.reshape(1, T),
-        surrogate.reshape(PAIRS, 128),
-        gain_cluster.reshape(1, D),
-        gain_summary.reshape(1, D),
-        w_query, w_key, w_value, w_out,
+        *(
+            pltpu.with_memory_space_constraint(arg, pltpu.HBM)
+            for arg in (
+                tokens_in,
+                dest_slot.reshape(1, T),
+                surrogate.reshape(PAIRS, 128),
+                gain_cluster.reshape(1, D),
+                gain_summary.reshape(1, D),
+                w_query, w_key, w_value,
+            )
+        )
     )
+    return jnp.dot(mixture, w_out, preferred_element_type=F32).astype(BF16)
 
 
 def solution(mesh):

time: 39.2 us -> 37.5 us (0.957)
  local copies, waits for them, and re-layouts: 1.67 us -> 0.01 us
  Pallas kernels: 37.4 us -> 36.2 us
  matrix products: 0 us -> 1.15 us
    unnamed x1 -> x2, local copies, waits for them, and re-layouts: 1.67 us -> 0.01 us
    dot_general x0 -> x1, matrix products: none -> 1.15 us  [body(): return jnp.dot(mixture, w_out, preferred_element_type=F32).astype(BF16)]
    pallas_call x1, Pallas kernels: 37.4 us -> 36.2 us  [body(): pl.pallas_call(kernel, out_shape=jax.ShapeDtypeStruct((T, D), BF16), in_s...]
where the time goes in v3:
time: 37.5 us; the launch traced here: 37.4 us
  Pallas kernels  36.2 us (97%)
  matrix products  1.15 us (3%)
    pallas_call x1, Pallas kernels, body(): pl.pallas_call(kernel, out_shape=jax.ShapeDtypeStruct((T, D), BF16), in_s...  36.2 us
    dot_general x1, matrix products, body(): return jnp.dot(mixture, w_out, preferred_element_type=F32).astype(BF16)  1.15 us

profile of v3, /device:TPU:1, one launch (start us, length us, event | category | flops | bytes accessed | tf_op | source)
XLA Modules:
  0.0 37.4 jit_solution(9094958978382790283)
XLA Ops:
  0.0 0.0 copy-start
  0.0 36.2 %shard_map.91 = bf16[128,1024]{1,0:T(8,128)(2,1)S(1)} custom-call(bf16[128,1024]{1,0:T(8,128)(2,1)} %x_hbm.1, s32[1,128]{1,0:T(1,128)} %bitcast.9, bf16[8,128]{1,0:T(8,128)(2,1)} %bitcast.8, f32[1,1024]{1,0:T(1,128)} %bitcast.6, f32[1,1024]{1,0:T(1,128)} %bitcast.7, bf16[1024,1024]{1,0:T(8,128)(2,1)} %wq_hbm.1, bf16[1024,1024]{1,0:T(8,128)(2,1)} %wk_hbm.1, ...), custom_call_target="tpu_custom_call" | custom-call | tf_op jit(solution)/shard_map/pallas_call | solution.py:286
  36.2 0.0 copy-done
  36.2 1.2 %convolution_convert_fusion = bf16[128,1024]{1,0:T(8,128)(2,1)} fusion(bf16[128,1024]{1,0:T(8,128)(2,1)S(1)} %shard_map.91, bf16[1024,1024]{1,0:T(8,128)(2,1)S(1)} %copy-done), kind=kOutput, calls=%fused_computation | convolution fusion | flops 268566528 | bytes 2621440 | tf_op jit(solution)/shard_map/dot_general | solution.py:326
Async XLA Ops:
  0.0 36.2 %copy-start = (bf16[1024,1024]{1,0:T(8,128)(2,1)S(1)}, bf16[1024,1024]{1,0:T(8,128)(2,1)}, u32[]{:S(2)}) copy-start(bf16[1024,1024]{1,0:T(8,128)(2,1)} %param.17) | copy-start | bytes 6291460

commit v4 on v3

--- a/solution.py
+++ b/solution.py
@@ -17,6 +17,8 @@
 D = 1024
 HEADS, HD = 16, 64
 PAIRS = D // 128
+FAR_FIRST = (2, 1, 3, 0)
+ROWS_FAR_FIRST = [(dy, dc) for dc in (1, 0) for dy in FAR_FIRST]
 CAP = 2
 ROWS = N * CAP
 PAD = 128.0
@@ -56,13 +58,23 @@
 def kernel(
     x_hbm, slot_hbm, surr_hbm, gain_c_hbm, gain_s_hbm, wq_hbm, wk_hbm, wv_hbm,
     out_ref,
-    x_ref, slot_ref, surr_ref, gain_c_ref, gain_s_ref, wq, wk, wv, stage, rows, send_buf, recv_buf, back_buf, home_buf, sum_buf, sums_buf, att, q_loc,
+    x_ref, slot_ref, surr_ref, gain_c_ref, gain_s_ref, wq, wk, wv, stage, rows, send_buf, recv_buf, back_buf, home_buf, sums_buf, att, q_loc,
     x_sem, w_sem, fwd_send, fwd_recv, sum_send, sum_recv, pass_send, pass_recv, back_send, back_recv, row_sem,
 ):
     gx, gy = lax.axis_index("gx"), lax.axis_index("gy")
-    me = gx * GY + gy
-
-    y, core = gx // 2, lax.rem(gx, 2)
+
+    y, core, x, z = gx // 2, lax.rem(gx, 2), gy // 4, lax.rem(gy, 4)
+
+    def far_first(i):
+        a, b = i // 4, lax.rem(i, 4)
+        tx = lax.rem(x + 2 + a * (a + 1) // 2, 4)
+        return tx * 4 + lax.rem(z + 2 + b * (b + 1) // 2, 4)
+
+    def row_at(dy, dc):
+        return lax.rem(y + 4 + dy, 4) * 2 + lax.rem(core + dc, 2)
+
+    mine = core * CHIPS + y * GY + gy
+
     firsts = [
         pltpu.make_async_copy(src, dst, x_sem.at[i])
         for i, (src, dst) in enumerate(((slot_hbm, slot_ref), (x_hbm, x_ref)))
@@ -91,7 +103,10 @@
             load.wait()
         for load in loads:
             load.start()
-        owner_row = (slot_ref[...] >> 7).astype(F32)
+        owner = slot_ref[...] >> 7
+        steps = ((owner >> 5) + (4 - y)) & 3
+        other = ((owner >> 4) + core) & 1
+        owner_row = (steps * 32 + other * GY + (owner & (GY - 1))).astype(F32)
         sub, lane = iota((T, T), 0), iota((T, T), 1)
         owner_wide = jnp.broadcast_to(owner_row, (T, T))
         owner_col = jnp.sum(jnp.where(sub == lane, owner_wide, 0.0), axis=1, keepdims=True)
@@ -112,21 +127,23 @@
             pl.semaphore_signal(row_sem, inc=1, device_id=(lax.rem(gx + i, GX), gy), device_id_type=MESH)
         pl.semaphore_wait(row_sem, GX - 1)
 
-    def to_all(src_of, dst, send_sem, recv_sem):
-        def send(i, carry):
-            tx = lax.rem(gx + i // GY, GX)
-            ty = lax.rem(gy + lax.rem(i, GY), GY)
-            pltpu.make_async_remote_copy(
-                src_ref=src_of(tx * GY + ty),
-                dst_ref=dst.at[me],
-                send_sem=send_sem,
-                recv_sem=recv_sem,
-                device_id=(tx, ty),
-                device_id_type=MESH,
-            ).start()
-            return carry
-
-        lax.fori_loop(1, N, send, 0)
+    def to_all(src, dst, send_sem, recv_sems, sign):
+        for dy, dc in ROWS_FAR_FIRST:
+
+            def send(i, carry, dy=dy, dc=dc):
+                ty = far_first(i)
+                pltpu.make_async_remote_copy(
+                    src_ref=src.at[(dy * 2 + dc) * GY + ty],
+                    dst_ref=dst.at[(dy * 2 + dc) * GY + gy],
+                    send_sem=send_sem,
+                    recv_sem=recv_sems.at[dy * 2 + dc],
+                    device_id=(row_at(sign * dy, dc), ty),
+                    device_id_type=MESH,
+                ).start()
+                return carry
+
+            lax.fori_loop(0, GY if dy + dc else GY - 1, send, 0)
+        dst[pl.ds(gy, 1)] = src[pl.ds(gy, 1)]
 
     def wait_for(buf, count, sem):
         some = buf.at[pl.ds(0, count)]
@@ -135,23 +152,36 @@
     def wait_all(buf, sem):
         wait_for(buf, N - 1, sem)
 
+    def unpack(buf, recv_sems):
+        for dy, dc in ROWS_FAR_FIRST:
+            g = dy * 2 + dc
+            wait_for(buf, GY - 1 if g == 0 else GY, recv_sems.at[g])
+            tiles = buf[g * GY : (g + 1) * GY].astype(F32).reshape(GY * 16, 128)
+            stage[g * GY * 16 : (g + 1) * GY * 16, :] = tiles
+            for j in range(PAIRS):
+                part = stage[pl.ds(g * GY * 16 + j, GY * CAP, stride=8), :]
+                rows[g * GY * CAP : (g + 1) * GY * CAP, j * 128 : (j + 1) * 128] = part.astype(BF16)
+
     with jax.named_scope("send_tokens"):
-        to_all(lambda d: send_buf.at[d], recv_buf, fwd_send, fwd_recv)
-    recv_buf[pl.ds(me, 1)] = send_buf[pl.ds(me, 1)]
+        to_all(send_buf, recv_buf, fwd_send, fwd_recv, 1)
 
     with jax.named_scope("local_query"):
         loads[0].wait()
         q_loc[...] = dot(x_ref[...], wq[...]).astype(BF16)
 
-    def unpack(buf):
-        stage[...] = buf[...].astype(F32).reshape(ROWS * 8, 128)
-        for j in range(PAIRS):
-            rows[:, j * 128 : (j + 1) * 128] = stage[pl.ds(j, ROWS, stride=8), :].astype(BF16)
-
-    with jax.named_scope("wait_tokens"):
-        wait_all(recv_buf, fwd_recv)
+    with jax.named_scope("pool_weights"):
+        own = lax.broadcasted_iota(jnp.int32, (HEADS, D), 1) // HD == lax.broadcasted_iota(
+            jnp.int32, (HEADS, D), 0
+        )
+        loads[3].wait()
+        surr = surr_ref[...].astype(F32)
+        surr = jnp.concatenate([surr[j : j + 1] for j in range(PAIRS)], axis=1)
+        anchor = jnp.where(own, jnp.broadcast_to(surr, (HEADS, D)), 0.0).astype(BF16)
+        loads[1].wait()
+        pool_w = dot_nt(anchor, wk[...]).astype(BF16)
+
     with jax.named_scope("unpack"):
-        unpack(recv_buf)
+        unpack(recv_buf, fwd_recv)
         real = (rows[:, :128].astype(F32) < 100.0).astype(BF16)
         r_sub, r_lane = iota((ROWS, ROWS), 0), iota((ROWS, ROWS), 1)
         mark = jnp.where(r_sub == r_lane, -MARK, 0.0)
@@ -162,22 +192,14 @@
         members = dot(gather, rows[...]).astype(BF16)
 
     with jax.named_scope("key_value"):
-        loads[1].wait()
+        logits = dot_nt(pool_w, members)
+        raised = jnp.exp2((logits - jnp.max(logits, axis=1, keepdims=True)) * EXP2_SCALE)
+        pooled = (raised / jnp.sum(raised, axis=1, keepdims=True)).astype(BF16)
         key = dot(members, wk[...]).astype(BF16)
         loads[2].wait()
         value = dot(members, wv[...]).astype(BF16)
 
     with jax.named_scope("summary"):
-        own = lax.broadcasted_iota(jnp.int32, (HEADS, D), 1) // HD == lax.broadcasted_iota(
-            jnp.int32, (HEADS, D), 0
-        )
-        loads[3].wait()
-        surr = surr_ref[...].astype(F32)
-        surr = jnp.concatenate([surr[j : j + 1] for j in range(PAIRS)], axis=1)
-        anchor = jnp.where(own, jnp.broadcast_to(surr, (HEADS, D)), 0.0).astype(BF16)
-        logits = dot_nt(anchor, key)
-        raised = jnp.exp2((logits - jnp.max(logits, axis=1, keepdims=True)) * EXP2_SCALE)
-        pooled = (raised / jnp.sum(raised, axis=1, keepdims=True)).astype(BF16)
         key_sum = jnp.where(own, dot(pooled, key), 0.0)
         key_sum = key_sum * lax.rsqrt(jnp.sum(key_sum * key_sum, axis=1, keepdims=True) / HD + 1e-6)
         key_sum = jnp.sum(key_sum, axis=0, keepdims=True)
@@ -185,25 +207,22 @@
         for j in range(PAIRS):
             stage[j : j + 1, :] = key_sum[:, j * 128 : (j + 1) * 128]
             stage[8 + j : 9 + j, :] = value_sum[:, j * 128 : (j + 1) * 128]
-        sum_buf[...] = stage[:16, :].astype(BF16)
+        sums_buf[pl.ds(mine, 1)] = stage[:16, :].astype(BF16)[None]
     with jax.named_scope("send_summary"):
-        mine = core * CHIPS + y * GY + gy
-        for dy in range(4):
+        for dy in FAR_FIRST:
 
             def send(i, carry, dy=dy):
-                tx, ty = lax.rem(gx + 2 * dy, GX), lax.rem(gy + i, GY)
                 pltpu.make_async_remote_copy(
-                    src_ref=sum_buf,
+                    src_ref=sums_buf.at[mine],
                     dst_ref=sums_buf.at[mine],
                     send_sem=sum_send,
                     recv_sem=sum_recv.at[dy],
-                    device_id=(tx, ty),
+                    device_id=(row_at(dy, 0), far_first(i)),
                     device_id_type=MESH,
                 ).start()
                 return carry
 
-            lax.fori_loop(1 if dy == 0 else 0, GY, send, 0)
-        sums_buf[pl.ds(mine, 1)] = sum_buf[...][None]
+            lax.fori_loop(0, GY if dy else GY - 1, send, 0)
 
     low = lax.broadcasted_iota(jnp.int32, (T, 128), 1) < HD
 
@@ -224,12 +243,11 @@
             stage[pl.ds(j, ROWS, stride=8), :] = dot(scatter, branch[:, j * 128 : (j + 1) * 128])
         back_buf[...] = stage[...].astype(BF16).reshape(N, 16, 128)
     with jax.named_scope("send_back"):
-        to_all(lambda d: back_buf.at[d], home_buf, back_send, back_recv)
-    home_buf[pl.ds(me, 1)] = back_buf[pl.ds(me, 1)]
+        to_all(back_buf, home_buf, back_send, back_recv, -1)
 
     with jax.named_scope("pass_summary"):
         passes = []
-        for dy in range(4):
+        for dy in FAR_FIRST:
             wait_for(sums_buf, GY - 1 if dy == 0 else GY, sum_recv.at[dy])
             block = sums_buf.at[pl.ds(core * CHIPS + lax.rem(y + 4 - dy, 4) * GY, GY)]
             passes.append(
@@ -262,10 +280,8 @@
         loads[5].wait()
         att[...] = att[...] * scale * gain_s_ref[...]
 
-    with jax.named_scope("wait_back"):
-        wait_all(home_buf, back_recv)
     with jax.named_scope("mix_out"):
-        unpack(home_buf)
+        unpack(home_buf, back_recv)
         pick_back = (iota((T, ROWS), 1) == place_col).astype(BF16)
         mixture = (dot(pick_back, rows[...]) + att[...]).astype(BF16)
         out_ref[...] = mixture
@@ -300,11 +316,10 @@
             pltpu.VMEM((ROWS * 8, 128), F32),
             pltpu.VMEM((ROWS, D), BF16),
             tiles, tiles, tiles, tiles,
-            pltpu.VMEM((16, 128), BF16),
             tiles,
             pltpu.VMEM((T, D), F32),
             pltpu.VMEM((T, D), BF16),
-            dma((2,)), dma((6,)), dma, dma, dma, dma((4,)), dma((4,)), dma((4,)), dma, dma,
+            dma((2,)), dma((6,)), dma, dma((GX,)), dma, dma((4,)), dma((4,)), dma((4,)), dma, dma((GX,)),
             pltpu.SemaphoreType.REGULAR,
         ],
         compiler_params=pltpu.CompilerParams(

time: 37.5 us -> 36.5 us (0.973); the launches traced: 37.4 us -> 35.8 us
  Pallas kernels: 36.2 us -> 34.6 us
    pallas_call x1, Pallas kernels: 36.2 us -> 34.6 us  [body(): pl.pallas_call(kernel, out_shape=jax.ShapeDtypeStruct((T, D), BF16), in_s...]
where the time goes in v4:
time: 36.5 us; the launch traced here: 35.8 us
  Pallas kernels  34.6 us (95%)
  matrix products  1.15 us (3%)
    pallas_call x1, Pallas kernels, body(): pl.pallas_call(kernel, out_shape=jax.ShapeDtypeStruct((T, D), BF16), in_s...  34.6 us
    dot_general x1, matrix products, body(): return jnp.dot(mixture, w_out, preferred_element_type=F32).astype(BF16)  1.15 us

profile of v4, /device:TPU:1, one launch (start us, length us, event | category | flops | bytes accessed | tf_op | source)
XLA Modules:
  0.0 35.8 jit_solution(18363505883848484484)
XLA Ops:
  0.0 0.0 copy-start
  0.0 34.6 %shard_map.91 = bf16[128,1024]{1,0:T(8,128)(2,1)S(1)} custom-call(bf16[128,1024]{1,0:T(8,128)(2,1)} %x_hbm.1, s32[1,128]{1,0:T(1,128)} %bitcast.9, bf16[8,128]{1,0:T(8,128)(2,1)} %bitcast.8, f32[1,1024]{1,0:T(1,128)} %bitcast.6, f32[1,1024]{1,0:T(1,128)} %bitcast.7, bf16[1024,1024]{1,0:T(8,128)(2,1)} %wq_hbm.1, bf16[1024,1024]{1,0:T(8,128)(2,1)} %wk_hbm.1, ...), custom_call_target="tpu_custom_call" | custom-call | tf_op jit(solution)/shard_map/pallas_call | solution.py:302
  34.7 0.0 copy-done
  34.7 1.2 %convolution_convert_fusion = bf16[128,1024]{1,0:T(8,128)(2,1)} fusion(bf16[128,1024]{1,0:T(8,128)(2,1)S(1)} %shard_map.91, bf16[1024,1024]{1,0:T(8,128)(2,1)S(1)} %copy-done), kind=kOutput, calls=%fused_computation | convolution fusion | flops 268566528 | bytes 2621440 | tf_op jit(solution)/shard_map/dot_general | solution.py:341
Async XLA Ops:
  0.0 34.7 %copy-start = (bf16[1024,1024]{1,0:T(8,128)(2,1)S(1)}, bf16[1024,1024]{1,0:T(8,128)(2,1)}, u32[]{:S(2)}) copy-start(bf16[1024,1024]{1,0:T(8,128)(2,1)} %param.17) | copy-start | bytes 6291460

commit v5 on v4

--- a/solution.py
+++ b/solution.py
@@ -59,16 +59,14 @@
     x_hbm, slot_hbm, surr_hbm, gain_c_hbm, gain_s_hbm, wq_hbm, wk_hbm, wv_hbm,
     out_ref,
     x_ref, slot_ref, surr_ref, gain_c_ref, gain_s_ref, wq, wk, wv, stage, rows, send_buf, recv_buf, back_buf, home_buf, sums_buf, att, q_loc,
-    x_sem, w_sem, fwd_send, fwd_recv, sum_send, sum_recv, pass_send, pass_recv, back_send, back_recv, row_sem,
+    x_sem, w_sem, fwd_send, fwd_recv, sum_send, sum_recv, pass_send, pass_recv, back_send, back_recv,
 ):
     gx, gy = lax.axis_index("gx"), lax.axis_index("gy")
 
     y, core, x, z = gx // 2, lax.rem(gx, 2), gy // 4, lax.rem(gy, 4)
 
-    def far_first(i):
-        a, b = i // 4, lax.rem(i, 4)
-        tx = lax.rem(x + 2 + a * (a + 1) // 2, 4)
-        return tx * 4 + lax.rem(z + 2 + b * (b + 1) // 2, 4)
+    xs = [lax.rem(x + d, 4) * 4 for d in range(4)]
+    zs = [lax.rem(z + d, 4) for d in range(4)]
 
     def row_at(dy, dc):
         return lax.rem(y + 4 + dy, 4) * 2 + lax.rem(core + dc, 2)
@@ -91,12 +89,15 @@
     for load in firsts:
         load.start()
 
-    with jax.named_scope("barrier_a"):
+    with jax.named_scope("barrier_signal"):
         barrier = pltpu.get_barrier_semaphore()
-        for i in range(1, GX):
-            pl.semaphore_signal(barrier, inc=1, device_id=(lax.rem(gx + i, GX), gy), device_id_type=MESH)
-        for i in range(1, GY):
-            pl.semaphore_signal(barrier, inc=1, device_id=(gx, lax.rem(gy + i, GY)), device_id_type=MESH)
+        for dy in FAR_FIRST:
+            for dx in FAR_FIRST:
+                for dz in FAR_FIRST:
+                    for dc in (1, 0):
+                        if dy or dx or dz or dc:
+                            there = (row_at(dy, dc), xs[dx] + zs[dz])
+                            pl.semaphore_signal(barrier, inc=1, device_id=there, device_id_type=MESH)
 
     with jax.named_scope("pack"):
         for load in firsts:
@@ -121,28 +122,24 @@
             stage[pl.ds(j, ROWS, stride=8), :] = jnp.where(filled, part, PAD)
         send_buf[...] = stage[...].astype(BF16).reshape(N, 16, 128)
 
-    with jax.named_scope("barrier_b"):
-        pl.semaphore_wait(barrier, GX + GY - 2)
-        for i in range(1, GX):
-            pl.semaphore_signal(row_sem, inc=1, device_id=(lax.rem(gx + i, GX), gy), device_id_type=MESH)
-        pl.semaphore_wait(row_sem, GX - 1)
+    with jax.named_scope("barrier_wait"):
+        pl.semaphore_wait(barrier, N - 1)
 
     def to_all(src, dst, send_sem, recv_sems, sign):
         for dy, dc in ROWS_FAR_FIRST:
-
-            def send(i, carry, dy=dy, dc=dc):
-                ty = far_first(i)
-                pltpu.make_async_remote_copy(
-                    src_ref=src.at[(dy * 2 + dc) * GY + ty],
-                    dst_ref=dst.at[(dy * 2 + dc) * GY + gy],
-                    send_sem=send_sem,
-                    recv_sem=recv_sems.at[dy * 2 + dc],
-                    device_id=(row_at(sign * dy, dc), ty),
-                    device_id_type=MESH,
-                ).start()
-                return carry
-
-            lax.fori_loop(0, GY if dy + dc else GY - 1, send, 0)
+            there = row_at(sign * dy, dc)
+            for dx in FAR_FIRST:
+                for dz in FAR_FIRST:
+                    if dy or dc or dx or dz:
+                        ty = xs[dx] + zs[dz]
+                        pltpu.make_async_remote_copy(
+                            src_ref=src.at[(dy * 2 + dc) * GY + ty],
+                            dst_ref=dst.at[(dy * 2 + dc) * GY + gy],
+                            send_sem=send_sem,
+                            recv_sem=recv_sems.at[dy * 2 + dc],
+                            device_id=(there, ty),
+                            device_id_type=MESH,
+                        ).start()
         dst[pl.ds(gy, 1)] = src[pl.ds(gy, 1)]
 
     def wait_for(buf, count, sem):
@@ -177,8 +174,8 @@
         surr = surr_ref[...].astype(F32)
         surr = jnp.concatenate([surr[j : j + 1] for j in range(PAIRS)], axis=1)
         anchor = jnp.where(own, jnp.broadcast_to(surr, (HEADS, D)), 0.0).astype(BF16)
-        loads[1].wait()
-        pool_w = dot_nt(anchor, wk[...]).astype(BF16)
+        for load in loads[1:3] + loads[4:]:
+            load.wait()
 
     with jax.named_scope("unpack"):
         unpack(recv_buf, fwd_recv)
@@ -192,11 +189,10 @@
         members = dot(gather, rows[...]).astype(BF16)
 
     with jax.named_scope("key_value"):
-        logits = dot_nt(pool_w, members)
+        key = dot(members, wk[...]).astype(BF16)
+        logits = dot_nt(anchor, key)
         raised = jnp.exp2((logits - jnp.max(logits, axis=1, keepdims=True)) * EXP2_SCALE)
         pooled = (raised / jnp.sum(raised, axis=1, keepdims=True)).astype(BF16)
-        key = dot(members, wk[...]).astype(BF16)
-        loads[2].wait()
         value = dot(members, wv[...]).astype(BF16)
 
     with jax.named_scope("summary"):
@@ -210,19 +206,18 @@
         sums_buf[pl.ds(mine, 1)] = stage[:16, :].astype(BF16)[None]
     with jax.named_scope("send_summary"):
         for dy in FAR_FIRST:
-
-            def send(i, carry, dy=dy):
-                pltpu.make_async_remote_copy(
-                    src_ref=sums_buf.at[mine],
-                    dst_ref=sums_buf.at[mine],
-                    send_sem=sum_send,
-                    recv_sem=sum_recv.at[dy],
-                    device_id=(row_at(dy, 0), far_first(i)),
-                    device_id_type=MESH,
-                ).start()
-                return carry
-
-            lax.fori_loop(0, GY if dy else GY - 1, send, 0)
+            there = row_at(dy, 0)
+            for dx in FAR_FIRST:
+                for dz in FAR_FIRST:
+                    if dy or dx or dz:
+                        pltpu.make_async_remote_copy(
+                            src_ref=sums_buf.at[mine],
+                            dst_ref=sums_buf.at[mine],
+                            send_sem=sum_send,
+                            recv_sem=sum_recv.at[dy],
+                            device_id=(there, xs[dx] + zs[dz]),
+                            device_id_type=MESH,
+                        ).start()
 
     low = lax.broadcasted_iota(jnp.int32, (T, 128), 1) < HD
 
@@ -236,7 +231,6 @@
             square = square + got * got
             att[:, at] = got
         scale = lax.rsqrt(jnp.sum(square, axis=1, keepdims=True) / D + 1e-6)
-        loads[4].wait()
         branch = (att[...] * scale * gain_c_ref[...]).astype(BF16)
     with jax.named_scope("pack_back"):
         for j in range(PAIRS):
@@ -277,7 +271,6 @@
             square = square + got * got
             att[:, at] = got
         scale = lax.rsqrt(jnp.sum(square, axis=1, keepdims=True) / D + 1e-6)
-        loads[5].wait()
         att[...] = att[...] * scale * gain_s_ref[...]
 
     with jax.named_scope("mix_out"):
@@ -320,7 +313,6 @@
             pltpu.VMEM((T, D), F32),
             pltpu.VMEM((T, D), BF16),
             dma((2,)), dma((6,)), dma, dma((GX,)), dma, dma((4,)), dma((4,)), dma((4,)), dma, dma((GX,)),
-            pltpu.SemaphoreType.REGULAR,
         ],
         compiler_params=pltpu.CompilerParams(
             collective_id=0, has_side_effects=True, vmem_limit_bytes=40 * 2**20

time: 36.5 us -> 34.4 us (0.942)
  the two profiles are of different devices: /device:TPU:1 before, /device:TPU:0 now
where the time goes in v5:
time: 34.4 us; the launch traced here: 34.3 us
  Pallas kernels  33.1 us (96%)
  matrix products  1.15 us (3%)
    pallas_call x1, Pallas kernels, body(): pl.pallas_call(kernel, out_shape=jax.ShapeDtypeStruct((T, D), BF16), in_s...  33.1 us
    dot_general x1, matrix products, body(): return jnp.dot(mixture, w_out, preferred_element_type=F32).astype(BF16)  1.15 us

profile of v5, /device:TPU:0, one launch (start us, length us, event | category | flops | bytes accessed | tf_op | source)
XLA Modules:
  0.0 34.3 jit_solution(14598143036707655886)
XLA Ops:
  0.0 0.0 copy-start
  0.0 33.1 %shard_map.91 = bf16[128,1024]{1,0:T(8,128)(2,1)S(1)} custom-call(bf16[128,1024]{1,0:T(8,128)(2,1)} %x_hbm.1, s32[1,128]{1,0:T(1,128)} %bitcast.9, bf16[8,128]{1,0:T(8,128)(2,1)} %bitcast.8, f32[1,1024]{1,0:T(1,128)} %bitcast.6, f32[1,1024]{1,0:T(1,128)} %bitcast.7, bf16[1024,1024]{1,0:T(8,128)(2,1)} %wq_hbm.1, bf16[1024,1024]{1,0:T(8,128)(2,1)} %wk_hbm.1, ...), custom_call_target="tpu_custom_call" | custom-call | tf_op jit(solution)/shard_map/pallas_call | solution.py:295
  33.2 0.0 copy-done
  33.2 1.2 %convolution_convert_fusion = bf16[128,1024]{1,0:T(8,128)(2,1)} fusion(bf16[128,1024]{1,0:T(8,128)(2,1)S(1)} %shard_map.91, bf16[1024,1024]{1,0:T(8,128)(2,1)S(1)} %copy-done), kind=kOutput, calls=%fused_computation | convolution fusion | flops 268566528 | bytes 2621440 | tf_op jit(solution)/shard_map/dot_general | solution.py:333
Async XLA Ops:
  0.0 33.2 %copy-start = (bf16[1024,1024]{1,0:T(8,128)(2,1)S(1)}, bf16[1024,1024]{1,0:T(8,128)(2,1)}, u32[]{:S(2)}) copy-start(bf16[1024,1024]{1,0:T(8,128)(2,1)} %param.17) | copy-start | bytes 6291460

commit v6 on v5

--- a/solution.py
+++ b/solution.py
@@ -56,9 +56,9 @@
 
 
 def kernel(
-    x_hbm, slot_hbm, surr_hbm, gain_c_hbm, gain_s_hbm, wq_hbm, wk_hbm, wv_hbm,
+    x_hbm, slot_hbm, surr_hbm, gain_c_hbm, gain_s_hbm, wq_hbm, wk_hbm, wv_hbm, wo_hbm,
     out_ref,
-    x_ref, slot_ref, surr_ref, gain_c_ref, gain_s_ref, wq, wk, wv, stage, rows, send_buf, recv_buf, back_buf, home_buf, sums_buf, att, q_loc,
+    x_ref, slot_ref, surr_ref, gain_c_ref, gain_s_ref, wq, wk, wv, wo, stage, rows, send_buf, recv_buf, back_buf, home_buf, sums_buf, att, q_loc,
     x_sem, w_sem, fwd_send, fwd_recv, sum_send, sum_recv, pass_send, pass_recv, back_send, back_recv,
 ):
     gx, gy = lax.axis_index("gx"), lax.axis_index("gy")
@@ -82,7 +82,7 @@
         for i, (src, dst) in enumerate(
             (
                 (wq_hbm, wq), (wk_hbm, wk), (wv_hbm, wv),
-                (surr_hbm, surr_ref), (gain_c_hbm, gain_c_ref), (gain_s_hbm, gain_s_ref),
+                (surr_hbm, surr_ref), (gain_c_hbm, gain_c_ref), (gain_s_hbm, gain_s_ref), (wo_hbm, wo),
             )
         )
     ]
@@ -232,6 +232,7 @@
             att[:, at] = got
         scale = lax.rsqrt(jnp.sum(square, axis=1, keepdims=True) / D + 1e-6)
         branch = (att[...] * scale * gain_c_ref[...]).astype(BF16)
+        branch = dot(branch, wo[...]).astype(BF16)
     with jax.named_scope("pack_back"):
         for j in range(PAIRS):
             stage[pl.ds(j, ROWS, stride=8), :] = dot(scatter, branch[:, j * 128 : (j + 1) * 128])
@@ -271,7 +272,8 @@
             square = square + got * got
             att[:, at] = got
         scale = lax.rsqrt(jnp.sum(square, axis=1, keepdims=True) / D + 1e-6)
-        att[...] = att[...] * scale * gain_s_ref[...]
+        summary = (att[...] * scale * gain_s_ref[...]).astype(BF16)
+        att[...] = dot(summary, wo[...])
 
     with jax.named_scope("mix_out"):
         unpack(home_buf, back_recv)
@@ -292,10 +294,10 @@
     tiles = pltpu.VMEM((N, 16, 128), BF16)
     weight = pltpu.VMEM((D, D), BF16)
     dma = pltpu.SemaphoreType.DMA
-    mixture = pl.pallas_call(
+    layer_out = pl.pallas_call(
         kernel,
         out_shape=jax.ShapeDtypeStruct((T, D), BF16),
-        in_specs=[hbm] * 8,
+        in_specs=[hbm] * 9,
         out_specs=vmem,
         scratch_shapes=[
             pltpu.VMEM((T, D), BF16),
@@ -304,7 +306,7 @@
             pltpu.VMEM((1, D), F32),
             pltpu.VMEM((1, D), F32),
         ]
-        + [weight] * 3
+        + [weight] * 4
         + [
             pltpu.VMEM((ROWS * 8, 128), F32),
             pltpu.VMEM((ROWS, D), BF16),
@@ -312,7 +314,7 @@
             tiles,
             pltpu.VMEM((T, D), F32),
             pltpu.VMEM((T, D), BF16),
-            dma((2,)), dma((6,)), dma, dma((GX,)), dma, dma((4,)), dma((4,)), dma((4,)), dma, dma((GX,)),
+            dma((2,)), dma((7,)), dma, dma((GX,)), dma, dma((4,)), dma((4,)), dma((4,)), dma, dma((GX,)),
         ],
         compiler_params=pltpu.CompilerParams(
             collective_id=0, has_side_effects=True, vmem_limit_bytes=40 * 2**20
@@ -326,11 +328,11 @@
                 surrogate.reshape(PAIRS, 128),
                 gain_cluster.reshape(1, D),
                 gain_summary.reshape(1, D),
-                w_query, w_key, w_value,
+                w_query, w_key, w_value, w_out,
             )
         )
     )
-    return jnp.dot(mixture, w_out, preferred_element_type=F32).astype(BF16)
+    return layer_out
 
 
 def solution(mesh):

time: 34.4 us -> 34 us (0.988)
  the two profiles are of different devices: /device:TPU:0 before, /device:TPU:1 now
where the time goes in v6:
time: 34 us; the launch traced here: 33.5 us
  Pallas kernels  32.8 us (96%)
  local copies, waits for them, and re-layouts  0.71 us (2%)
    pallas_call x1, Pallas kernels, body(): pl.pallas_call(kernel, out_shape=jax.ShapeDtypeStruct((T, D), BF16), in_s...  32.8 us
    unnamed x1, local copies, waits for them, and re-layouts  0.71 us

profile of v6, /device:TPU:1, one launch (start us, length us, event | category | flops | bytes accessed | tf_op | source)
XLA Modules:
  0.0 33.5 jit_solution(11879207412851737807)
XLA Ops:
  0.0 32.8 %shard_map.91 = bf16[128,1024]{1,0:T(8,128)(2,1)S(1)} custom-call(bf16[128,1024]{1,0:T(8,128)(2,1)} %x_hbm.1, s32[1,128]{1,0:T(1,128)} %bitcast.7, bf16[8,128]{1,0:T(8,128)(2,1)} %bitcast.6, f32[1,1024]{1,0:T(1,128)} %bitcast.4, f32[1,1024]{1,0:T(1,128)} %bitcast.5, bf16[1024,1024]{1,0:T(8,128)(2,1)} %wq_hbm.1, bf16[1024,1024]{1,0:T(8,128)(2,1)} %wk_hbm.1, ...), custom_call_target="tpu_custom_call" | custom-call | tf_op jit(solution)/shard_map/pallas_call | solution.py:297
  32.8 0.7 %copy.11 = bf16[128,1024]{1,0:T(8,128)(2,1)} copy(bf16[128,1024]{1,0:T(8,128)(2,1)S(1)} %shard_map.91) | data formatting | bytes 524288

commit v7 on v6

--- a/solution.py
+++ b/solution.py
@@ -91,13 +91,13 @@
 
     with jax.named_scope("barrier_signal"):
         barrier = pltpu.get_barrier_semaphore()
-        for dy in FAR_FIRST:
-            for dx in FAR_FIRST:
-                for dz in FAR_FIRST:
-                    for dc in (1, 0):
-                        if dy or dx or dz or dc:
-                            there = (row_at(dy, dc), xs[dx] + zs[dz])
-                            pl.semaphore_signal(barrier, inc=1, device_id=there, device_id_type=MESH)
+        everyone = [
+            (dy, dx, dz, dc) for dy in FAR_FIRST for dx in FAR_FIRST for dz in FAR_FIRST for dc in (1, 0)
+        ]
+        for dy, dx, dz, dc in sorted(everyone, key=lambda d: -sum(min(v, 4 - v) for v in d[:3])):
+            if dy or dx or dz or dc:
+                there = (row_at(dy, dc), xs[dx] + zs[dz])
+                pl.semaphore_signal(barrier, inc=1, device_id=there, device_id_type=MESH)
 
     with jax.named_scope("pack"):
         for load in firsts:

time: 34 us -> 33.9 us (level)
  no operation moved by 1% of the time
where the time goes in v7:
time: 33.9 us; the launch traced here: 33.3 us
  Pallas kernels  32.6 us (96%)
  local copies, waits for them, and re-layouts  0.71 us (2%)
    pallas_call x1, Pallas kernels, body(): pl.pallas_call(kernel, out_shape=jax.ShapeDtypeStruct((T, D), BF16), in_s...  32.6 us
    unnamed x1, local copies, waits for them, and re-layouts  0.71 us

profile of v7, /device:TPU:1, one launch (start us, length us, event | category | flops | bytes accessed | tf_op | source)
XLA Modules:
  0.0 33.3 jit_solution(7286517241232410621)
XLA Ops:
  0.0 32.6 %shard_map.91 = bf16[128,1024]{1,0:T(8,128)(2,1)S(1)} custom-call(bf16[128,1024]{1,0:T(8,128)(2,1)} %x_hbm.1, s32[1,128]{1,0:T(1,128)} %bitcast.7, bf16[8,128]{1,0:T(8,128)(2,1)} %bitcast.6, f32[1,1024]{1,0:T(1,128)} %bitcast.4, f32[1,1024]{1,0:T(1,128)} %bitcast.5, bf16[1024,1024]{1,0:T(8,128)(2,1)} %wq_hbm.1, bf16[1024,1024]{1,0:T(8,128)(2,1)} %wk_hbm.1, ...), custom_call_target="tpu_custom_call" | custom-call | tf_op jit(solution)/shard_map/pallas_call | solution.py:297
  32.6 0.7 %copy.11 = bf16[128,1024]{1,0:T(8,128)(2,1)} copy(bf16[128,1024]{1,0:T(8,128)(2,1)S(1)} %shard_map.91) | data formatting | bytes 524288
